TPU v7x, 32 devices: a whole 2x2x4 slice. The times are simulated.
32 devices in a mesh: members: 2 (over x), wide: 8 (over z, y), narrow: 2 (over core).
Axes of the slice: x: 2, y: 2, z: 4, core: 2. Of those that a mesh axis runs over, the one named last changes fastest.
Arguments:
- coarse: bfloat16 [128, 128, 128], P(('members', 'wide')), parts along dimension 0, may hold values from -6 to 6
- wanted: int32 [8, 2, 8, 2], P('wide', 'narrow'), may hold values from -1 to 7, as said below
- intersection: int32 [512, 2, 4], P('wide', 'narrow'), may hold values from 0 to 15, as said below
- intersection_count: int32 [512, 2], P('wide', 'narrow'), may hold values from 1 to 4
- regrid_weight: bfloat16 [1024, 256, 4, 128], P('wide', 'narrow'), may hold values from -0.25 to 0.25
- reference_patch: bfloat16 [64, 512, 128], P(('wide', 'narrow')), may hold values from -300 to 300
- patch_index: int32 [256, 2], P('wide', 'narrow'), may hold values from 0 to 7
- query_weight: bfloat16 [128, 128], replicated, may hold values from -1 to 1
- key_value_weight: bfloat16 [128, 256], replicated, may hold values from -0.5 to 0.5
- out_weight: bfloat16 [128, 128], replicated, may hold values from -0.5 to 0.5
- conv_one: bfloat16 [3, 3, 128, 128], replicated, may hold values from -0.1875 to 0.1875
- conv_two: bfloat16 [3, 3, 128, 128], replicated, may hold values from -0.1875 to 0.1875
- gain_one: float32 [128], replicated, may hold values from 0.25 to 1.75
- gain_two: float32 [128], replicated, may hold values from 0.25 to 1.75
- gain_out: float32 [128], replicated, may hold values from 0.25 to 1.75
Outputs:
- fine_out: bfloat16 [2048, 256, 128], P(('members', 'wide'), 'narrow'), parts along dimension 0
There are 2 independent parts, one for each index of `members`. A program takes and returns all parts, laid end to end along the dimension named above; an argument that names none is the same for every part. Nothing has to cross between parts.
Inputs may be any that keep to these rules, and one draw needn't show every extreme that they name: `wanted`: each entry is a block number held by holder o, or -1 for an empty slot; the live numbers of one (w, n, o) are distinct and come first; in every draw some (w, n, o) fill all 2 slots. `intersection`: every entry names a slot o * 2 + s whose wanted[w, n, o, s] is not -1, where w and n are the wide and narrow indices of the fine block.
All inputs are finite; a program needn't handle non-finite values.
Results may differ from a plain program's by a relative error of at most 0.012.
The roundings to bfloat16 on the way count: a program that leaves them out, or rounds other values in their place, can miss the bound.
Values may be sent and summed in bfloat16 or wider, within the bound.
A program may use at most 256 MiB of HBM per device.

v0:
```python
import functools
import math

import jax
import jax.numpy as jnp
from jax import lax
from jax.experimental import pallas as pl
from jax.experimental.pallas import tpu as pltpu
from jax.sharding import PartitionSpec as P

BR = 2
AR = 4
SIDE = 16
LOG2E = 1.4426950408889634


def rms_scaled(values, scale_gain):
    mean_square = jnp.mean(values * values, axis=-1, keepdims=True)
    return values * lax.rsqrt(mean_square + 1e-06) * scale_gain


def silu(values):
    half = values * 0.5
    return half + half * jnp.tanh(half)


def attend_kernel(
    wanted,
    lists,
    counts,
    patches,
    weight,
    blocks,
    patch,
    query_weight,
    key_value_weight,
    out_weight,
    gain,
    carried,
    active,
    keys,
    values,
    *,
    per_step,
    entries,
    slots,
    held,
    fine_cols,
):
    step = pl.program_id(0)
    channels = blocks.shape[2]

    @pl.when(step == 0)
    def _():
        def one(index, carry):
            cells = patch[index]
            keys[index] = lax.dot_general(
                key_value_weight[:, :channels],
                cells,
                (((0,), (1,)), ((), ())),
                preferred_element_type=jnp.float32,
            ).astype(jnp.bfloat16)
            values[index, :, :channels] = jnp.dot(
                cells, key_value_weight[:, channels:], preferred_element_type=jnp.float32
            ).astype(jnp.bfloat16)
            values[index, :, channels:] = jnp.ones(cells.shape, jnp.bfloat16)
            return carry

        lax.fori_loop(0, patch.shape[0], one, 0)

    band_cells = BR * fine_cols
    tile_cells = AR * fine_cols
    bands = AR // BR
    factor = LOG2E / math.sqrt(channels)
    for local in range(per_step):
        tile = step * per_step + local
        pieces = []
        for band in range(bands):
            row = tile * bands + band
            used = counts[row]
            first = local * tile_cells + band * band_cells
            stacked = []
            for entry in range(entries):
                listed = lists[row * entries + entry]
                block = (listed // slots) * held + jnp.maximum(wanted[listed], 0)
                cells = blocks[block]
                stacked.append(jnp.where(entry < used, cells, jnp.zeros_like(cells)))
            spread = jnp.concatenate(
                [weight[first : first + band_cells, entry, :] for entry in range(entries)], axis=1
            )
            pieces.append(
                jnp.dot(
                    spread, jnp.concatenate(stacked, axis=0), preferred_element_type=jnp.float32
                ).astype(jnp.bfloat16)
            )
        regridded = jnp.concatenate(pieces, axis=0)
        queries = jnp.dot(
            regridded, query_weight[...], preferred_element_type=jnp.float32
        ).astype(jnp.bfloat16)
        chosen = patches[tile]
        scores = jnp.dot(queries, keys[chosen], preferred_element_type=jnp.float32)
        peak = jnp.max(scores, axis=-1, keepdims=True)
        lifted = jnp.exp2((scores - peak) * factor).astype(jnp.bfloat16)
        summed = jnp.dot(lifted, values[chosen], preferred_element_type=jnp.float32)
        attended = (summed[:, :channels] / summed[:, channels:]).astype(jnp.bfloat16)
        mixed = jnp.dot(attended, out_weight[...], preferred_element_type=jnp.float32)
        total = (regridded.astype(jnp.float32) + mixed).astype(jnp.bfloat16)
        where_to = pl.ds(local * tile_cells, tile_cells)
        carried[where_to, :] = total
        active[where_to, :] = silu(
            rms_scaled(total.astype(jnp.float32), gain[...])
        ).astype(jnp.bfloat16)


def attend(
    wanted, lists, counts, patches, weight, blocks, patch, query_weight, key_value_weight,
    out_weight, gain, held, slots, fine_cols,
):
    cells, entries, _ = weight.shape
    channels = blocks.shape[2]
    tile_cells = AR * fine_cols
    per_step = 2
    step_cells = per_step * tile_cells
    smem = pl.BlockSpec(memory_space=pltpu.SMEM)
    vmem = pl.BlockSpec(memory_space=pltpu.VMEM)
    out = jax.ShapeDtypeStruct((cells, channels), jnp.bfloat16)
    out_spec = pl.BlockSpec((step_cells, channels), lambda s: (s, 0))
    return pl.pallas_call(
        functools.partial(
            attend_kernel,
            per_step=per_step,
            entries=entries,
            slots=slots,
            held=held,
            fine_cols=fine_cols,
        ),
        grid=(cells // step_cells,),
        out_shape=(out, out),
        in_specs=[smem] * 4
        + [pl.BlockSpec((step_cells, entries, weight.shape[2]), lambda s: (s, 0, 0))]
        + [vmem] * 6,
        out_specs=(out_spec, out_spec),
        scratch_shapes=[
            pltpu.VMEM((patch.shape[0], channels, patch.shape[1]), jnp.bfloat16),
            pltpu.VMEM((patch.shape[0], patch.shape[1], 2 * channels), jnp.bfloat16),
        ],
        compiler_params=pltpu.CompilerParams(vmem_limit_bytes=48 * 1024 * 1024),
        name="attend",
    )(
        wanted, lists, counts, patches, weight, blocks, patch, query_weight, key_value_weight,
        out_weight, gain,
    )


def spread_taps(taps, wide_taps):
    channels = taps.shape[2]
    wide_taps[...] = jnp.zeros(wide_taps.shape, wide_taps.dtype)
    for column in range(3):
        for row in range(3):
            for out_row in range(2):
                wide_taps[
                    column,
                    (row + out_row) * channels : (row + out_row + 1) * channels,
                    out_row * channels : (out_row + 1) * channels,
                ] = taps[row, column]


def convolve(source, first, rows, wide_taps):
    width, channels = source.shape[1:]
    pairs = rows // 2
    slabs = [source[first + index] for index in range(rows + 2)]
    stacked = jnp.concatenate(
        [
            jnp.concatenate([slabs[2 * pair + shift] for shift in range(4)], axis=1)
            for pair in range(pairs)
        ],
        axis=0,
    )
    total = None
    for column, turn in ((1, 0), (0, 1), (2, width - 1)):
        part = jnp.dot(stacked, wide_taps[column], preferred_element_type=jnp.float32)
        part = part.reshape(pairs, width, 2 * channels)
        if turn:
            part = pltpu.roll(part, turn, 1)
        total = part if total is None else total + part
    return total


def conv_kernel(
    active, above, below, side, carried, taps_one, taps_two, gain_two, gain_out, out,
    padded, second, wide_one, wide_two, *, rows_one, rows_two,
):
    fine_rows, fine_cols, channels = active.shape
    width = padded.shape[1]
    spread_taps(taps_one, wide_one)
    spread_taps(taps_two, wide_two)
    padded[0:2, :fine_cols, :] = above[...]
    padded[fine_rows + 2 : fine_rows + 4, :fine_cols, :] = below[...]
    padded[:, fine_cols:, :] = side[...]

    def fill(index, carry):
        first = index * 8
        padded[pl.ds(first + 2, 8), :fine_cols, :] = active[pl.ds(first, 8)]
        return carry

    lax.fori_loop(0, fine_rows // 8, fill, 0)
    band = lax.axis_index("wide")
    part = lax.axis_index("narrow")
    column = lax.broadcasted_iota(jnp.int32, (1, width, channels), 1)
    left = (part > 0).astype(jnp.int32)
    right = (part < lax.axis_size("narrow") - 1).astype(jnp.int32)
    keep = (column < fine_cols + right) | (column >= width - left)

    def first_conv(index, carry):
        first = index * rows_one
        total = convolve(padded, first, rows_one, wide_one)
        for half in range(2):
            piece = total[:, :, half * channels : (half + 1) * channels]
            piece = silu(rms_scaled(piece, gain_two[...]))
            piece = jnp.where(keep, piece, 0.0).astype(jnp.bfloat16)
            for pair in range(rows_one // 2):
                second[first + 2 * pair + half] = piece[pair]
        return carry

    lax.fori_loop(0, (fine_rows + 2) // rows_one, first_conv, 0)

    @pl.when(band == 0)
    def _():
        second[0] = jnp.zeros((width, channels), jnp.bfloat16)

    @pl.when(band == lax.axis_size("wide") - 1)
    def _():
        second[fine_rows + 1] = jnp.zeros((width, channels), jnp.bfloat16)

    def second_conv(index, carry):
        first = index * rows_two
        total = convolve(second, first, rows_two, wide_two)
        for half in range(2):
            for pair in range(rows_two // 2):
                row = first + 2 * pair + half
                piece = total[pair, :fine_cols, half * channels : (half + 1) * channels]
                piece = piece + carried[row].astype(jnp.float32)
                out[row] = rms_scaled(piece, gain_out[...]).astype(jnp.bfloat16)
        return carry

    lax.fori_loop(0, fine_rows // rows_two, second_conv, 0)


def convolutions(active, above, below, side, carried, taps_one, taps_two, gain_two, gain_out):
    fine_rows, fine_cols, channels = active.shape
    width = fine_cols + SIDE
    vmem = pl.BlockSpec(memory_space=pltpu.VMEM)
    return pl.pallas_call(
        functools.partial(conv_kernel, rows_one=10, rows_two=8),
        out_shape=jax.ShapeDtypeStruct(active.shape, jnp.bfloat16),
        in_specs=[vmem] * 9,
        out_specs=vmem,
        scratch_shapes=[
            pltpu.VMEM((fine_rows + 4, width, channels), jnp.bfloat16),
            pltpu.VMEM((fine_rows + 2, width, channels), jnp.bfloat16),
            pltpu.VMEM((3, 4 * channels, 2 * channels), jnp.bfloat16),
            pltpu.VMEM((3, 4 * channels, 2 * channels), jnp.bfloat16),
        ],
        compiler_params=pltpu.CompilerParams(vmem_limit_bytes=56 * 1024 * 1024),
        name="convolutions",
    )(active, above, below, side, carried, taps_one, taps_two, gain_two, gain_out)


def from_both(cells, axis, dim, width):
    count = lax.axis_size(axis)
    ends = count - 1
    head = lax.slice_in_dim(cells, 0, width, axis=dim)
    tail = lax.slice_in_dim(cells, cells.shape[dim] - width, cells.shape[dim], axis=dim)
    before = lax.ppermute(tail, axis, [(i, i + 1) for i in range(ends)])
    after = lax.ppermute(head, axis, [(i + 1, i) for i in range(ends)])
    return before, after


def on_device(
    coarse,
    wanted,
    intersection,
    intersection_count,
    regrid_weight,
    reference_patch,
    patch_index,
    query_weight,
    key_value_weight,
    out_weight,
    conv_one,
    conv_two,
    gain_one,
    gain_two,
    gain_out,
):
    slot_count = wanted.shape[3]
    channels = coarse.shape[2]
    fine_rows, fine_cols, entries, block_cells = regrid_weight.shape
    every_block = lax.all_gather(coarse, "wide", axis=0, tiled=True)
    group_patch = lax.all_gather(reference_patch, "narrow", axis=0, tiled=True)
    carried, active = attend(
        wanted.reshape(-1),
        intersection.reshape(-1),
        intersection_count.reshape(-1),
        patch_index.reshape(-1),
        regrid_weight.reshape(fine_rows * fine_cols, entries, block_cells),
        every_block,
        group_patch,
        query_weight,
        key_value_weight,
        out_weight,
        gain_one.reshape(1, channels),
        coarse.shape[0],
        slot_count,
        fine_cols,
    )
    carried = carried.reshape(fine_rows, fine_cols, channels)
    active = active.reshape(fine_rows, fine_cols, channels)
    above, below = from_both(active, "wide", 0, 2)
    edges = jnp.concatenate(
        [
            jnp.concatenate([rows[:, :2], rows[:, fine_cols - 2 :]], axis=1)
            for rows in (above, active, below)
        ],
        axis=0,
    )
    before, after = from_both(edges, "narrow", 1, 2)
    middle = jnp.zeros((fine_rows + 4, SIDE - 4, channels), jnp.bfloat16)
    side = jnp.concatenate([after, middle, before], axis=1)
    return convolutions(
        active,
        above,
        below,
        side,
        carried,
        conv_one,
        conv_two,
        gain_two.reshape(1, channels),
        gain_out.reshape(1, channels),
    )


def solution(mesh):
    placed = (
        P(("members", "wide"), None, None),
        P("wide", "narrow", None, None),
        P("wide", "narrow", None),
        P("wide", "narrow"),
        P("wide", "narrow", None, None),
        P(("wide", "narrow"), None, None),
        P("wide", "narrow"),
        P(),
        P(),
        P(),
        P(),
        P(),
        P(),
        P(),
        P(),
    )
    return jax.shard_map(
        on_device,
        mesh=mesh,
        in_specs=placed,
        out_specs=P(("members", "wide"), "narrow", None),
        check_vma=False,
    )
```

profile of v0, /device:TPU:0, one launch (start us, length us, event | category | flops | bytes accessed | tf_op | source)
XLA Modules:
  0.0 197.4 jit_solution(5214832669733824308)
XLA Ops:
  6.5 0.0 all-gather.5.cloned.1.call-start
  6.5 0.7 all-gather.5.cloned.1.call-update
  7.3 0.0 all-gather.3.cloned.1.call-start
  7.3 0.7 all-gather.3.cloned.1.call-update
  8.0 0.8 copy.19
  8.8 0.1 reshape.32.wanted
  8.8 0.8 copy.20
  9.6 0.1 reshape.33.lists
  9.7 11.0 %all-gather.5.cloned.1.call-done.patch = bf16[8,512,128]{2,1,0:T(8,128)(2,1)} async-done(((bf16[4,512,128]{2,1,0:T(8,128)(2,1)}), bf16[8,512,128]{2,1,0:T(8,128)(2,1)}) %all-gather.5.cloned.1.call-update) | async-done | bytes 1048592 | tf_op jit(solution)/shard_map/all_gather | solution.py:300
  20.7 52.6 %all-gather.3.cloned.1.call-done.blocks = bf16[64,128,128]{2,1,0:T(8,128)(2,1)} async-done(((bf16[8,128,128]{2,1,0:T(8,128)(2,1)}), bf16[64,128,128]{2,1,0:T(8,128)(2,1)}) %all-gather.3.cloned.1.call-update) | async-done | bytes 2097168 | tf_op jit(solution)/shard_map/all_gather | solution.py:299
  73.3 0.0 copy-start
  73.3 1.6 copy-done
  74.9 0.0 copy-start.1
  74.9 1.2 copy-done.1
  76.1 0.0 copy-start.2
  76.1 0.8 copy-done.2
  76.9 0.0 copy-start.3
  76.9 0.8 copy-done.3
  77.7 0.0 copy-start.4
  77.7 0.8 copy-done.4
  78.5 0.0 copy-start.5
  78.5 0.7 copy-done.5
  79.1 0.0 copy-start.6
  79.1 0.7 copy-done.6
  79.8 0.0 copy-start.7
  79.8 0.7 copy-done.7
  80.4 60.1 %attend.1 = (bf16[16384,128]{1,0:T(8,128)(2,1)}, bf16[16384,128]{1,0:T(8,128)(2,1)}) custom-call(s32[16]{0:T(128)S(1)} %reshape.32.wanted, s32[256]{0:T(256)S(1)} %reshape.33.lists, s32[64]{0:T(128)S(1)} %bitcast.14, s32[32]{0:T(128)S(1)} %bitcast.15, bf16[16384,4,128]{2,1,0:T(4,128)(2,1)} %bitcast.17, bf16[64,128,128]{2,1,0:T(8,128)(2,1)S(1)} %copy-done, ...), custom_call_target="tpu_custom_call" | custom-call | tf_op jit(solution)/shard_map/attend/pallas_call | solution.py:128
  140.5 0.9 fusion.1
  141.4 2.5 %collective-permute-start = (bf16[2,128,128]{2,1,0:T(8,128)(2,1)S(1)}, bf16[2,128,128]{2,1,0:T(8,128)(2,1)S(1)}, u32[]{:S(2)}, u32[]{:S(2)}) collective-permute-start(bf16[2,128,128]{2,1,0:T(8,128)(2,1)S(1)} %bitcast.22), channel_id=1, source_target_pairs={{0,2},{2,4},{4,6},{6,8},{8,10},{10,12},{12,14},{1,3},{3,5},{5,7},{... | collective-permute-start | bytes 196616 | tf_op jit(solution)/shard_map/ppermute | solution.py:274
  143.9 1.1 fusion
  145.0 1.3 collective-permute-start.1
  146.3 0.0 collective-permute-done.above
  146.3 0.0 copy-start.8
  146.3 5.2 %collective-permute-done.1.below = bf16[2,128,128]{2,1,0:T(8,128)(2,1)S(1)} collective-permute-done((bf16[2,128,128]{2,1,0:T(8,128)(2,1)S(1)}, bf16[2,128,128]{2,1,0:T(8,128)(2,1)S(1)}, u32[]{:S(2)}, u32[]{:S(2)}) %collective-permute-start.1) | collective-permute-done | bytes 65568 | tf_op jit(solution)/shard_map/ppermute | solution.py:275
  151.5 0.0 copy-start.9
  151.6 0.1 maximum_maximum_fusion
  151.7 0.1 fusion.2
  151.8 1.3 collective-permute-start.2
  153.1 3.0 %collective-permute-start.3 = (bf16[132,2,128]{2,1,0:T(2,128)(2,1)S(1)}, bf16[132,2,128]{2,1,0:T(2,128)(2,1)S(1)}, u32[]{:S(2)}, u32[]{:S(2)}) collective-permute-start(bf16[132,2,128]{2,1,0:T(2,128)(2,1)S(1)} %get-tuple-element.14), channel_id=1, source_target_pairs={{0,1},{2,3},{4,5},{6,7},{8,9},{10,11},{12,13},{14,15},{16,17},{18,... | collective-permute-start | bytes 202760 | tf_op jit(solution)/shard_map/ppermute | solution.py:274
  156.2 0.1 pad.1.clone
  156.2 0.0 collective-permute-done.2
  156.3 0.8 collective-permute-done.3
  157.0 1.1 pad_maximum_fusion.side
  158.1 0.0 copy-done.8
  158.1 0.0 copy-done.9
  158.1 32.4 %convolutions.1 = bf16[128,128,128]{2,1,0:T(8,128)(2,1)} custom-call(bf16[128,128,128]{2,1,0:T(8,128)(2,1)} %bitcast.19, bf16[2,128,128]{2,1,0:T(8,128)(2,1)} %copy-done.8, bf16[2,128,128]{2,1,0:T(8,128)(2,1)} %copy-done.9, bf16[132,16,128]{2,1,0:T(8,128)(2,1)} %pad_maximum_fusion.side, bf16[128,128,128]{2,1,0:T(8,128)(2,1)} %bitcast.20, ...), custom_call_target="tpu_custom_call" | custom-call | tf_op jit(solution)/shard_map/convolutions/pallas_call | solution.py:253
  (3 shorter events, 0.0 us)
Async XLA Ops:
  6.5 14.1 %all-gather.5.cloned.1.call-start = ((), (), s32[]{:S(2)}) async-start(), calls=%async_computation.1 | async-start | bytes 1572864 | tf_op jit(solution)/shard_map/all_gather | solution.py:300
  7.3 66.0 %all-gather.3.cloned.1.call-start = ((), (), s32[]{:S(2)}) async-start(), calls=%async_computation | async-start | bytes 2359296 | tf_op jit(solution)/shard_map/all_gather | solution.py:299
  73.3 1.6 copy-start
  74.9 1.2 copy-start.1
  76.1 0.8 copy-start.2
  76.9 0.8 copy-start.3
  77.7 0.8 copy-start.4
  78.5 0.7 copy-start.5
  79.1 0.7 copy-start.6
  79.8 0.7 copy-start.7
  141.4 4.9 %collective-permute-start = (bf16[2,128,128]{2,1,0:T(8,128)(2,1)S(1)}, bf16[2,128,128]{2,1,0:T(8,128)(2,1)S(1)}, u32[]{:S(2)}, u32[]{:S(2)}) collective-permute-start(bf16[2,128,128]{2,1,0:T(8,128)(2,1)S(1)} %bitcast.22), channel_id=1, source_target_pairs={{0,2},{2,4},{4,6},{6,8},{8,10},{10,12},{12,14},{1,3},{3,5},{5,7},{... | collective-permute-start | bytes 196616 | tf_op jit(solution)/shard_map/ppermute | solution.py:274
  145.0 6.5 %collective-permute-start.1 = (bf16[2,128,128]{2,1,0:T(8,128)(2,1)S(1)}, bf16[2,128,128]{2,1,0:T(8,128)(2,1)S(1)}, u32[]{:S(2)}, u32[]{:S(2)}) collective-permute-start(bf16[2,128,128]{2,1,0:T(8,128)(2,1)S(1)} %bitcast.21), channel_id=1, source_target_pairs={{2,0},{4,2},{6,4},{8,6},{10,8},{12,10},{14,12},{3,1},{5,3},{7,5},{... | collective-permute-start | bytes 196616 | tf_op jit(solution)/shard_map/ppermute | solution.py:275
  146.3 11.8 %copy-start.8 = (bf16[2,128,128]{2,1,0:T(8,128)(2,1)}, bf16[2,128,128]{2,1,0:T(8,128)(2,1)S(1)}, u32[]{:S(2)}) copy-start(bf16[2,128,128]{2,1,0:T(8,128)(2,1)S(1)} %collective-permute-done.above) | copy-start | bytes 196612
  151.5 6.6 %copy-start.9 = (bf16[2,128,128]{2,1,0:T(8,128)(2,1)}, bf16[2,128,128]{2,1,0:T(8,128)(2,1)S(1)}, u32[]{:S(2)}) copy-start(bf16[2,128,128]{2,1,0:T(8,128)(2,1)S(1)} %collective-permute-done.1.below) | copy-start | bytes 196612
  151.8 4.4 %collective-permute-start.2 = (bf16[132,2,128]{2,1,0:T(2,128)(2,1)S(1)}, bf16[132,2,128]{2,1,0:T(2,128)(2,1)S(1)}, u32[]{:S(2)}, u32[]{:S(2)}) collective-permute-start(bf16[132,2,128]{2,1,0:T(2,128)(2,1)S(1)} %get-tuple-element.13), channel_id=1, source_target_pairs={{1,0},{3,2},{5,4},{7,6},{9,8},{11,10},{13,12},{15,14},{17,16},{19,... | collective-permute-start | bytes 202760 | tf_op jit(solution)/shard_map/ppermute | solution.py:275
  153.1 3.9 %collective-permute-start.3 = (bf16[132,2,128]{2,1,0:T(2,128)(2,1)S(1)}, bf16[132,2,128]{2,1,0:T(2,128)(2,1)S(1)}, u32[]{:S(2)}, u32[]{:S(2)}) collective-permute-start(bf16[132,2,128]{2,1,0:T(2,128)(2,1)S(1)} %get-tuple-element.14), channel_id=1, source_target_pairs={{0,1},{2,3},{4,5},{6,7},{8,9},{10,11},{12,13},{14,15},{16,17},{18,... | collective-permute-start | bytes 202760 | tf_op jit(solution)/shard_map/ppermute | solution.py:274
Sparse Core Ops, SparseCore 0:
  8.9 11.7 all-gather.4
  22.8 50.4 all-gather.2
where the time goes:
time: 198 us; the launch traced here: 197 us
  Pallas kernels  92.5 us (47%)
  waiting for transfers between devices  71 us (36%)
  between operations  13.5 us (7%)
  local copies, waits for them, and re-layouts  11.1 us (6%)
  starting transfers between devices  8.12 us (4%)
    pallas_call x1, Pallas kernels, attend(): pl.pallas_call(functools.partial(attend_kernel, per_step=per_step, entrie...  60.1 us
    all_gather x1, waiting for transfers between devices, on_device(): every_block = lax.all_gather(coarse, 'wide', axis=0, tiled=True)  52.6 us
    pallas_call x1, Pallas kernels, convolutions(): pl.pallas_call(functools.partial(conv_kernel, rows_one=10, rows_two=8), o...  32.4 us
    all_gather x1, waiting for transfers between devices, on_device(): group_patch = lax.all_gather(reference_patch, 'narrow', axis=0, tiled=True)  11 us
    unnamed x22, local copies, waits for them, and re-layouts  8.67 us
    ppermute x2, starting transfers between devices, from_both(): before = lax.ppermute(tail, axis, [(i, i + 1) for i in range(ends)])  5.49 us
    ppermute x2, waiting for transfers between devices, from_both(): after = lax.ppermute(head, axis, [(i + 1, i) for i in range(ends)])  5.21 us
  transfers between devices with their start and end apart: 6, of which 4 were waited for; matrix products, arithmetic and copies ran while one was open for 1% of the time, Pallas kernels for 0%

commit v1 on v0

--- a/solution.py
+++ b/solution.py
@@ -22,6 +22,131 @@
 def silu(values):
     half = values * 0.5
     return half + half * jnp.tanh(half)
+
+
+def gather_kernel(
+    coarse, patch, blocks, patches, send_right, send_left, recv_right, recv_left,
+    pass_send, pass_recv, patch_sem, own_sem,
+):
+    ring = lax.axis_size("wide")
+    held = coarse.shape[0]
+    share = held // 2
+    group = patch.shape[0]
+    here = lax.axis_index("wide")
+    core = lax.axis_index("narrow")
+    level = here // 2
+    place = level + (here % 2) * (ring - 1 - 2 * level)
+
+    def index_of(spot):
+        upper = spot // (ring // 2)
+        return 2 * spot + upper * (2 * ring - 1 - 4 * spot)
+
+    right = {"wide": index_of((place + 1) % ring)}
+    left = {"wide": index_of((place + ring - 1) % ring)}
+    other = {"narrow": 1 - core}
+    barrier = pltpu.get_barrier_semaphore()
+    for target in (right, left, other):
+        pl.semaphore_signal(
+            barrier, inc=1, device_id=target, device_id_type=pl.DeviceIdType.MESH
+        )
+    pl.semaphore_wait(barrier, 3)
+
+    def rows(spot):
+        return pl.ds(index_of(spot) * held + core * share, share)
+
+    def send(source, target, send_sem, recv_sem, device):
+        return pltpu.make_async_remote_copy(
+            src_ref=source,
+            dst_ref=target,
+            send_sem=send_sem,
+            recv_sem=recv_sem,
+            device_id=device,
+            device_id_type=pl.DeviceIdType.MESH,
+        )
+
+    right_steps, left_steps = ring // 2, (ring - 1) // 2
+    own = coarse.at[pl.ds(core * share, share)]
+    mine = blocks.at[rows(place)]
+    going_right = [send(own, mine, send_right.at[0], recv_right.at[0], right)]
+    going_left = [send(own, mine, send_left.at[0], recv_left.at[0], left)]
+    going_right[0].start()
+    going_left[0].start()
+    across = send(
+        patch,
+        patches.at[pl.ds(core * group, group)],
+        patch_sem.at[0],
+        patch_sem.at[1],
+        other,
+    )
+    across.start()
+    own_blocks = pltpu.make_async_copy(coarse, blocks.at[pl.ds(here * held, held)], own_sem.at[0])
+    own_blocks.start()
+    own_patch = pltpu.make_async_copy(
+        patch, patches.at[pl.ds(core * group, group)], own_sem.at[1]
+    )
+    own_patch.start()
+    passed = []
+    for step in range(right_steps):
+        going_right[step].wait_recv()
+        landed = blocks.at[rows((place + ring - 1 - step) % ring)]
+        if step + 1 < right_steps:
+            copy = send(
+                landed, landed, send_right.at[step + 1], recv_right.at[step + 1], right
+            )
+            copy.start()
+            going_right.append(copy)
+        copy = send(landed, landed, pass_send.at[len(passed)], pass_recv.at[len(passed)], other)
+        copy.start()
+        passed.append(copy)
+        if step < left_steps:
+            going_left[step].wait_recv()
+            landed = blocks.at[rows((place + 1 + step) % ring)]
+            if step + 1 < left_steps:
+                copy = send(
+                    landed, landed, send_left.at[step + 1], recv_left.at[step + 1], left
+                )
+                copy.start()
+                going_left.append(copy)
+            copy = send(
+                landed, landed, pass_send.at[len(passed)], pass_recv.at[len(passed)], other
+            )
+            copy.start()
+            passed.append(copy)
+    for copy in going_right + going_left:
+        copy.wait_send()
+    for copy in passed:
+        copy.wait()
+    across.wait()
+    own_blocks.wait()
+    own_patch.wait()
+
+
+def gather(coarse, patch):
+    ring = lax.axis_size("wide")
+    right_steps, left_steps = ring // 2, (ring - 1) // 2
+    dma = pltpu.SemaphoreType.DMA
+    anywhere = pl.BlockSpec(memory_space=pl.ANY)
+    return pl.pallas_call(
+        gather_kernel,
+        out_shape=(
+            jax.ShapeDtypeStruct((ring * coarse.shape[0],) + coarse.shape[1:], coarse.dtype),
+            jax.ShapeDtypeStruct((2 * patch.shape[0],) + patch.shape[1:], patch.dtype),
+        ),
+        in_specs=[anywhere] * 2,
+        out_specs=(anywhere, anywhere),
+        scratch_shapes=[
+            dma((right_steps,)),
+            dma((left_steps,)),
+            dma((right_steps,)),
+            dma((left_steps,)),
+            dma((ring - 1,)),
+            dma((ring - 1,)),
+            dma((2,)),
+            dma((2,)),
+        ],
+        compiler_params=pltpu.CompilerParams(collective_id=0, has_side_effects=True),
+        name="gather",
+    )(coarse, patch)
 
 
 def attend_kernel(
@@ -296,8 +421,7 @@
     slot_count = wanted.shape[3]
     channels = coarse.shape[2]
     fine_rows, fine_cols, entries, block_cells = regrid_weight.shape
-    every_block = lax.all_gather(coarse, "wide", axis=0, tiled=True)
-    group_patch = lax.all_gather(reference_patch, "narrow", axis=0, tiled=True)
+    every_block, group_patch = gather(coarse, reference_patch)
     carried, active = attend(
         wanted.reshape(-1),
         intersection.reshape(-1),

time: 198 us -> 147 us (0.74)
  waiting for transfers between devices: 71 us -> 4.47 us
  Pallas kernels: 92.5 us -> 121 us
  between operations: 13.5 us -> 0.12 us
    all_gather x2 -> x0, waiting for transfers between devices: 63.6 us -> none  [the longest x1 52.6 us: on_device(): every_block = lax.all_gather(coarse, 'wide', axis=0, tiled=True)]
    pallas_call x0 -> x1, Pallas kernels: none -> 28.3 us  [gather(): pl.pallas_call(gather_kernel, out_shape=(jax.ShapeDtypeStruct((ring * coa...]
  transfers between devices with their start and end apart: 6 -> 4, of which waited for: 4 -> 2; matrix products, arithmetic and copies ran while one was open for 1% -> 1% of each run, Pallas kernels for 0% -> 0%
where the time goes in v1:
time: 147 us
  Pallas kernels  121 us (82%)
  local copies, waits for them, and re-layouts  11.1 us (8%)
  starting transfers between devices  9.04 us (6%)
  waiting for transfers between devices  4.47 us (3%)
    pallas_call x1, Pallas kernels, attend(): pl.pallas_call(functools.partial(attend_kernel, per_step=per_step, entrie...  60.1 us
    pallas_call x1, Pallas kernels, convolutions(): pl.pallas_call(functools.partial(conv_kernel, rows_one=10, rows_two=8), o...  32.5 us
    pallas_call x1, Pallas kernels, gather(): pl.pallas_call(gather_kernel, out_shape=(jax.ShapeDtypeStruct((ring * coa...  28.3 us
    unnamed x22, local copies, waits for them, and re-layouts  8.66 us
    ppermute x2, starting transfers between devices, from_both(): before = lax.ppermute(tail, axis, [(i, i + 1) for i in range(ends)])  6.45 us
    ppermute x2, waiting for transfers between devices, from_both(): after = lax.ppermute(head, axis, [(i + 1, i) for i in range(ends)])  3.68 us
  transfers between devices with their start and end apart: 4, of which 2 were waited for; matrix products, arithmetic and copies ran while one was open for 1% of the time, Pallas kernels for 0%

profile of v1, /device:TPU:0, one launch (start us, length us, event | category | flops | bytes accessed | tf_op | source)
XLA Modules:
  0.0 146.8 jit_solution(1295762812523180689)
XLA Ops:
  0.0 0.8 copy.17
  0.8 0.1 reshape.32.wanted
  0.8 0.8 copy.18
  1.6 0.1 reshape.33.lists
  1.7 28.3 %gather.1 = (bf16[64,128,128]{2,1,0:T(8,128)(2,1)}, bf16[8,512,128]{2,1,0:T(8,128)(2,1)}) custom-call(bf16[8,128,128]{2,1,0:T(8,128)(2,1)} %coarse.1, bf16[4,512,128]{2,1,0:T(8,128)(2,1)} %patch.1), custom_call_target="tpu_custom_call" | custom-call | tf_op jit(solution)/shard_map/gather/pallas_call | solution.py:129
  30.0 0.0 copy-start
  30.0 1.6 %copy-done = bf16[64,128,128]{2,1,0:T(8,128)(2,1)S(1)} copy-done((bf16[64,128,128]{2,1,0:T(8,128)(2,1)S(1)}, bf16[64,128,128]{2,1,0:T(8,128)(2,1)}, u32[]{:S(2)}) %copy-start) | copy-done | bytes 2097176
  31.6 0.0 copy-start.1
  31.6 1.2 copy-done.1
  32.8 0.0 copy-start.2
  32.8 0.8 copy-done.2
  33.7 0.0 copy-start.3
  33.7 0.8 copy-done.3
  34.4 0.0 copy-start.4
  34.4 0.8 copy-done.4
  35.2 0.0 copy-start.5
  35.2 0.7 copy-done.5
  35.9 0.0 copy-start.6
  35.9 0.7 copy-done.6
  36.5 0.0 copy-start.7
  36.5 0.7 copy-done.7
  37.2 60.1 %attend.1 = (bf16[16384,128]{1,0:T(8,128)(2,1)}, bf16[16384,128]{1,0:T(8,128)(2,1)}) custom-call(s32[16]{0:T(128)S(1)} %reshape.32.wanted, s32[256]{0:T(256)S(1)} %reshape.33.lists, s32[64]{0:T(128)S(1)} %bitcast.14, s32[32]{0:T(128)S(1)} %bitcast.15, bf16[16384,4,128]{2,1,0:T(4,128)(2,1)} %bitcast.17, bf16[64,128,128]{2,1,0:T(8,128)(2,1)S(1)} %copy-done, ...), custom_call_target="tpu_custom_call" | custom-call | tf_op jit(solution)/shard_map/attend/pallas_call | solution.py:253
  97.3 0.9 fusion.1
  98.1 3.4 %collective-permute-start = (bf16[2,128,128]{2,1,0:T(8,128)(2,1)S(1)}, bf16[2,128,128]{2,1,0:T(8,128)(2,1)S(1)}, u32[]{:S(2)}, u32[]{:S(2)}) collective-permute-start(bf16[2,128,128]{2,1,0:T(8,128)(2,1)S(1)} %bitcast.22), channel_id=1, source_target_pairs={{0,2},{2,4},{4,6},{6,8},{8,10},{10,12},{12,14},{1,3},{3,5},{5,7},{... | collective-permute-start | bytes 196616 | tf_op jit(solution)/shard_map/ppermute | solution.py:399
  101.6 1.3 collective-permute-start.1
  102.9 1.1 fusion
  104.0 0.0 collective-permute-done.above
  104.0 0.0 copy-start.8
  104.0 3.7 %collective-permute-done.1.below = bf16[2,128,128]{2,1,0:T(8,128)(2,1)S(1)} collective-permute-done((bf16[2,128,128]{2,1,0:T(8,128)(2,1)S(1)}, bf16[2,128,128]{2,1,0:T(8,128)(2,1)S(1)}, u32[]{:S(2)}, u32[]{:S(2)}) %collective-permute-start.1) | collective-permute-done | bytes 65568 | tf_op jit(solution)/shard_map/ppermute | solution.py:400
  107.7 0.0 copy-start.9
  107.7 0.1 maximum_maximum_fusion
  107.9 0.1 fusion.2
  108.0 1.3 collective-permute-start.2
  109.3 3.0 %collective-permute-start.3 = (bf16[132,2,128]{2,1,0:T(2,128)(2,1)S(1)}, bf16[132,2,128]{2,1,0:T(2,128)(2,1)S(1)}, u32[]{:S(2)}, u32[]{:S(2)}) collective-permute-start(bf16[132,2,128]{2,1,0:T(2,128)(2,1)S(1)} %get-tuple-element.18), channel_id=1, source_target_pairs={{0,1},{2,3},{4,5},{6,7},{8,9},{10,11},{12,13},{14,15},{16,17},{18,... | collective-permute-start | bytes 202760 | tf_op jit(solution)/shard_map/ppermute | solution.py:399
  112.3 0.1 pad.1.clone
  112.4 0.0 collective-permute-done.2
  112.4 0.8 collective-permute-done.3
  113.2 1.1 pad_maximum_fusion.side
  114.3 0.0 copy-done.8
  114.3 0.0 copy-done.9
  114.3 32.5 %convolutions.1 = bf16[128,128,128]{2,1,0:T(8,128)(2,1)} custom-call(bf16[128,128,128]{2,1,0:T(8,128)(2,1)} %bitcast.19, bf16[2,128,128]{2,1,0:T(8,128)(2,1)} %copy-done.8, bf16[2,128,128]{2,1,0:T(8,128)(2,1)} %copy-done.9, bf16[132,16,128]{2,1,0:T(8,128)(2,1)} %pad_maximum_fusion.side, bf16[128,128,128]{2,1,0:T(8,128)(2,1)} %bitcast.20, ...), custom_call_target="tpu_custom_call" | custom-call | tf_op jit(solution)/shard_map/convolutions/pallas_call | solution.py:378
  (3 shorter events, 0.0 us)
Async XLA Ops:
  30.0 1.6 %copy-start = (bf16[64,128,128]{2,1,0:T(8,128)(2,1)S(1)}, bf16[64,128,128]{2,1,0:T(8,128)(2,1)}, u32[]{:S(2)}) copy-start(bf16[64,128,128]{2,1,0:T(8,128)(2,1)} %get-tuple-element.9.blocks) | copy-start | bytes 6291460
  31.6 1.2 copy-start.1
  32.8 0.8 copy-start.2
  33.7 0.8 copy-start.3
  34.4 0.8 copy-start.4
  35.2 0.7 copy-start.5
  35.9 0.7 copy-start.6
  36.5 0.7 copy-start.7
  98.1 5.9 %collective-permute-start = (bf16[2,128,128]{2,1,0:T(8,128)(2,1)S(1)}, bf16[2,128,128]{2,1,0:T(8,128)(2,1)S(1)}, u32[]{:S(2)}, u32[]{:S(2)}) collective-permute-start(bf16[2,128,128]{2,1,0:T(8,128)(2,1)S(1)} %bitcast.22), channel_id=1, source_target_pairs={{0,2},{2,4},{4,6},{6,8},{8,10},{10,12},{12,14},{1,3},{3,5},{5,7},{... | collective-permute-start | bytes 196616 | tf_op jit(solution)/shard_map/ppermute | solution.py:399
  101.6 6.2 %collective-permute-start.1 = (bf16[2,128,128]{2,1,0:T(8,128)(2,1)S(1)}, bf16[2,128,128]{2,1,0:T(8,128)(2,1)S(1)}, u32[]{:S(2)}, u32[]{:S(2)}) collective-permute-start(bf16[2,128,128]{2,1,0:T(8,128)(2,1)S(1)} %bitcast.21), channel_id=1, source_target_pairs={{2,0},{4,2},{6,4},{8,6},{10,8},{12,10},{14,12},{3,1},{5,3},{7,5},{... | collective-permute-start | bytes 196616 | tf_op jit(solution)/shard_map/ppermute | solution.py:400
  104.0 10.3 %copy-start.8 = (bf16[2,128,128]{2,1,0:T(8,128)(2,1)}, bf16[2,128,128]{2,1,0:T(8,128)(2,1)S(1)}, u32[]{:S(2)}) copy-start(bf16[2,128,128]{2,1,0:T(8,128)(2,1)S(1)} %collective-permute-done.above) | copy-start | bytes 196612
  107.7 6.6 %copy-start.9 = (bf16[2,128,128]{2,1,0:T(8,128)(2,1)}, bf16[2,128,128]{2,1,0:T(8,128)(2,1)S(1)}, u32[]{:S(2)}) copy-start(bf16[2,128,128]{2,1,0:T(8,128)(2,1)S(1)} %collective-permute-done.1.below) | copy-start | bytes 196612
  108.0 4.4 %collective-permute-start.2 = (bf16[132,2,128]{2,1,0:T(2,128)(2,1)S(1)}, bf16[132,2,128]{2,1,0:T(2,128)(2,1)S(1)}, u32[]{:S(2)}, u32[]{:S(2)}) collective-permute-start(bf16[132,2,128]{2,1,0:T(2,128)(2,1)S(1)} %get-tuple-element.17), channel_id=1, source_target_pairs={{1,0},{3,2},{5,4},{7,6},{9,8},{11,10},{13,12},{15,14},{17,16},{19,... | collective-permute-start | bytes 202760 | tf_op jit(solution)/shard_map/ppermute | solution.py:400
  109.3 3.9 %collective-permute-start.3 = (bf16[132,2,128]{2,1,0:T(2,128)(2,1)S(1)}, bf16[132,2,128]{2,1,0:T(2,128)(2,1)S(1)}, u32[]{:S(2)}, u32[]{:S(2)}) collective-permute-start(bf16[132,2,128]{2,1,0:T(2,128)(2,1)S(1)} %get-tuple-element.18), channel_id=1, source_target_pairs={{0,1},{2,3},{4,5},{6,7},{8,9},{10,11},{12,13},{14,15},{16,17},{18,... | collective-permute-start | bytes 202760 | tf_op jit(solution)/shard_map/ppermute | solution.py:399

commit v2 on v1

--- a/solution.py
+++ b/solution.py
@@ -210,8 +210,11 @@
                 block = (listed // slots) * held + jnp.maximum(wanted[listed], 0)
                 cells = blocks[block]
                 stacked.append(jnp.where(entry < used, cells, jnp.zeros_like(cells)))
-            spread = jnp.concatenate(
-                [weight[first : first + band_cells, entry, :] for entry in range(entries)], axis=1
+            spread = (
+                weight[first : first + band_cells]
+                .astype(jnp.float32)
+                .reshape(band_cells, entries * weight.shape[2])
+                .astype(jnp.bfloat16)
             )
             pieces.append(
                 jnp.dot(

time: 147 us -> 129 us (0.88)
  Pallas kernels: 121 us -> 102 us
    pallas_call x1, Pallas kernels: 60.1 us -> 41.3 us  [attend(): pl.pallas_call(functools.partial(attend_kernel, per_step=per_step, entrie...]
where the time goes in v2:
time: 129 us; the launch traced here: 128 us
  Pallas kernels  102 us (79%)
  local copies, waits for them, and re-layouts  11.1 us (9%)
  starting transfers between devices  9.04 us (7%)
  waiting for transfers between devices  4.47 us (3%)
    pallas_call x1, Pallas kernels, attend(): pl.pallas_call(functools.partial(attend_kernel, per_step=per_step, entrie...  41.3 us
    pallas_call x1, Pallas kernels, convolutions(): pl.pallas_call(functools.partial(conv_kernel, rows_one=10, rows_two=8), o...  32.5 us
    pallas_call x1, Pallas kernels, gather(): pl.pallas_call(gather_kernel, out_shape=(jax.ShapeDtypeStruct((ring * coa...  28.3 us
    unnamed x22, local copies, waits for them, and re-layouts  8.66 us
    ppermute x2, starting transfers between devices, from_both(): before = lax.ppermute(tail, axis, [(i, i + 1) for i in range(ends)])  6.45 us
    ppermute x2, waiting for transfers between devices, from_both(): after = lax.ppermute(head, axis, [(i + 1, i) for i in range(ends)])  3.68 us
    ppermute x2, starting transfers between devices, from_both(): after = lax.ppermute(head, axis, [(i + 1, i) for i in range(ends)])  2.58 us
  transfers between devices with their start and end apart: 4, of which 2 were waited for; matrix products, arithmetic and copies ran while one was open for 1% of the time, Pallas kernels for 0%

profile of v2, /device:TPU:0, one launch (start us, length us, event | category | flops | bytes accessed | tf_op | source)
XLA Modules:
  0.0 128.0 jit_solution(16475964528558833566)
XLA Ops:
  0.0 0.8 copy.17
  0.8 0.1 reshape.32.wanted
  0.8 0.8 copy.18
  1.6 0.1 reshape.33.lists
  1.7 28.3 %gather.1 = (bf16[64,128,128]{2,1,0:T(8,128)(2,1)}, bf16[8,512,128]{2,1,0:T(8,128)(2,1)}) custom-call(bf16[8,128,128]{2,1,0:T(8,128)(2,1)} %coarse.1, bf16[4,512,128]{2,1,0:T(8,128)(2,1)} %patch.1), custom_call_target="tpu_custom_call" | custom-call | tf_op jit(solution)/shard_map/gather/pallas_call | solution.py:129
  30.0 0.0 copy-start
  30.0 1.6 %copy-done = bf16[64,128,128]{2,1,0:T(8,128)(2,1)S(1)} copy-done((bf16[64,128,128]{2,1,0:T(8,128)(2,1)S(1)}, bf16[64,128,128]{2,1,0:T(8,128)(2,1)}, u32[]{:S(2)}) %copy-start) | copy-done | bytes 2097176
  31.6 0.0 copy-start.1
  31.6 1.2 copy-done.1
  32.8 0.0 copy-start.2
  32.8 0.8 copy-done.2
  33.7 0.0 copy-start.3
  33.7 0.8 copy-done.3
  34.4 0.0 copy-start.4
  34.4 0.8 copy-done.4
  35.2 0.0 copy-start.5
  35.2 0.7 copy-done.5
  35.9 0.0 copy-start.6
  35.9 0.7 copy-done.6
  36.5 0.0 copy-start.7
  36.5 0.7 copy-done.7
  37.2 41.3 %attend.1 = (bf16[16384,128]{1,0:T(8,128)(2,1)}, bf16[16384,128]{1,0:T(8,128)(2,1)}) custom-call(s32[16]{0:T(128)S(1)} %reshape.32.wanted, s32[256]{0:T(256)S(1)} %reshape.33.lists, s32[64]{0:T(128)S(1)} %bitcast.14, s32[32]{0:T(128)S(1)} %bitcast.15, bf16[16384,4,128]{2,1,0:T(4,128)(2,1)} %bitcast.17, bf16[64,128,128]{2,1,0:T(8,128)(2,1)S(1)} %copy-done, ...), custom_call_target="tpu_custom_call" | custom-call | tf_op jit(solution)/shard_map/attend/pallas_call | solution.py:256
  78.4 0.9 fusion.1
  79.3 3.4 %collective-permute-start = (bf16[2,128,128]{2,1,0:T(8,128)(2,1)S(1)}, bf16[2,128,128]{2,1,0:T(8,128)(2,1)S(1)}, u32[]{:S(2)}, u32[]{:S(2)}) collective-permute-start(bf16[2,128,128]{2,1,0:T(8,128)(2,1)S(1)} %bitcast.22), channel_id=1, source_target_pairs={{0,2},{2,4},{4,6},{6,8},{8,10},{10,12},{12,14},{1,3},{3,5},{5,7},{... | collective-permute-start | bytes 196616 | tf_op jit(solution)/shard_map/ppermute | solution.py:402
  82.7 1.3 %collective-permute-start.1 = (bf16[2,128,128]{2,1,0:T(8,128)(2,1)S(1)}, bf16[2,128,128]{2,1,0:T(8,128)(2,1)S(1)}, u32[]{:S(2)}, u32[]{:S(2)}) collective-permute-start(bf16[2,128,128]{2,1,0:T(8,128)(2,1)S(1)} %bitcast.21), channel_id=1, source_target_pairs={{2,0},{4,2},{6,4},{8,6},{10,8},{12,10},{14,12},{3,1},{5,3},{7,5},{... | collective-permute-start | bytes 196616 | tf_op jit(solution)/shard_map/ppermute | solution.py:403
  84.0 1.1 fusion
  85.2 0.0 collective-permute-done.above
  85.2 0.0 copy-start.8
  85.2 3.7 %collective-permute-done.1.below = bf16[2,128,128]{2,1,0:T(8,128)(2,1)S(1)} collective-permute-done((bf16[2,128,128]{2,1,0:T(8,128)(2,1)S(1)}, bf16[2,128,128]{2,1,0:T(8,128)(2,1)S(1)}, u32[]{:S(2)}, u32[]{:S(2)}) %collective-permute-start.1) | collective-permute-done | bytes 65568 | tf_op jit(solution)/shard_map/ppermute | solution.py:403
  88.9 0.0 copy-start.9
  88.9 0.1 maximum_maximum_fusion
  89.1 0.1 fusion.2
  89.2 1.3 %collective-permute-start.2 = (bf16[132,2,128]{2,1,0:T(2,128)(2,1)S(1)}, bf16[132,2,128]{2,1,0:T(2,128)(2,1)S(1)}, u32[]{:S(2)}, u32[]{:S(2)}) collective-permute-start(bf16[132,2,128]{2,1,0:T(2,128)(2,1)S(1)} %get-tuple-element.17), channel_id=1, source_target_pairs={{1,0},{3,2},{5,4},{7,6},{9,8},{11,10},{13,12},{15,14},{17,16},{19,... | collective-permute-start | bytes 202760 | tf_op jit(solution)/shard_map/ppermute | solution.py:403
  90.5 3.0 %collective-permute-start.3 = (bf16[132,2,128]{2,1,0:T(2,128)(2,1)S(1)}, bf16[132,2,128]{2,1,0:T(2,128)(2,1)S(1)}, u32[]{:S(2)}, u32[]{:S(2)}) collective-permute-start(bf16[132,2,128]{2,1,0:T(2,128)(2,1)S(1)} %get-tuple-element.18), channel_id=1, source_target_pairs={{0,1},{2,3},{4,5},{6,7},{8,9},{10,11},{12,13},{14,15},{16,17},{18,... | collective-permute-start | bytes 202760 | tf_op jit(solution)/shard_map/ppermute | solution.py:402
  93.5 0.1 pad.1.clone
  93.6 0.0 collective-permute-done.2
  93.6 0.8 collective-permute-done.3
  94.4 1.1 pad_maximum_fusion.side
  95.5 0.0 copy-done.8
  95.5 0.0 copy-done.9
  95.5 32.5 %convolutions.1 = bf16[128,128,128]{2,1,0:T(8,128)(2,1)} custom-call(bf16[128,128,128]{2,1,0:T(8,128)(2,1)} %bitcast.19, bf16[2,128,128]{2,1,0:T(8,128)(2,1)} %copy-done.8, bf16[2,128,128]{2,1,0:T(8,128)(2,1)} %copy-done.9, bf16[132,16,128]{2,1,0:T(8,128)(2,1)} %pad_maximum_fusion.side, bf16[128,128,128]{2,1,0:T(8,128)(2,1)} %bitcast.20, ...), custom_call_target="tpu_custom_call" | custom-call | tf_op jit(solution)/shard_map/convolutions/pallas_call | solution.py:381
  (3 shorter events, 0.0 us)
Async XLA Ops:
  30.0 1.6 %copy-start = (bf16[64,128,128]{2,1,0:T(8,128)(2,1)S(1)}, bf16[64,128,128]{2,1,0:T(8,128)(2,1)}, u32[]{:S(2)}) copy-start(bf16[64,128,128]{2,1,0:T(8,128)(2,1)} %get-tuple-element.9.blocks) | copy-start | bytes 6291460
  31.6 1.2 copy-start.1
  32.8 0.8 copy-start.2
  33.7 0.8 copy-start.3
  34.4 0.8 copy-start.4
  35.2 0.7 copy-start.5
  35.9 0.7 copy-start.6
  36.5 0.7 copy-start.7
  79.3 5.9 %collective-permute-start = (bf16[2,128,128]{2,1,0:T(8,128)(2,1)S(1)}, bf16[2,128,128]{2,1,0:T(8,128)(2,1)S(1)}, u32[]{:S(2)}, u32[]{:S(2)}) collective-permute-start(bf16[2,128,128]{2,1,0:T(8,128)(2,1)S(1)} %bitcast.22), channel_id=1, source_target_pairs={{0,2},{2,4},{4,6},{6,8},{8,10},{10,12},{12,14},{1,3},{3,5},{5,7},{... | collective-permute-start | bytes 196616 | tf_op jit(solution)/shard_map/ppermute | solution.py:402
  82.7 6.2 %collective-permute-start.1 = (bf16[2,128,128]{2,1,0:T(8,128)(2,1)S(1)}, bf16[2,128,128]{2,1,0:T(8,128)(2,1)S(1)}, u32[]{:S(2)}, u32[]{:S(2)}) collective-permute-start(bf16[2,128,128]{2,1,0:T(8,128)(2,1)S(1)} %bitcast.21), channel_id=1, source_target_pairs={{2,0},{4,2},{6,4},{8,6},{10,8},{12,10},{14,12},{3,1},{5,3},{7,5},{... | collective-permute-start | bytes 196616 | tf_op jit(solution)/shard_map/ppermute | solution.py:403
  85.2 10.3 %copy-start.8 = (bf16[2,128,128]{2,1,0:T(8,128)(2,1)}, bf16[2,128,128]{2,1,0:T(8,128)(2,1)S(1)}, u32[]{:S(2)}) copy-start(bf16[2,128,128]{2,1,0:T(8,128)(2,1)S(1)} %collective-permute-done.above) | copy-start | bytes 196612
  88.9 6.6 %copy-start.9 = (bf16[2,128,128]{2,1,0:T(8,128)(2,1)}, bf16[2,128,128]{2,1,0:T(8,128)(2,1)S(1)}, u32[]{:S(2)}) copy-start(bf16[2,128,128]{2,1,0:T(8,128)(2,1)S(1)} %collective-permute-done.1.below) | copy-start | bytes 196612
  89.2 4.4 %collective-permute-start.2 = (bf16[132,2,128]{2,1,0:T(2,128)(2,1)S(1)}, bf16[132,2,128]{2,1,0:T(2,128)(2,1)S(1)}, u32[]{:S(2)}, u32[]{:S(2)}) collective-permute-start(bf16[132,2,128]{2,1,0:T(2,128)(2,1)S(1)} %get-tuple-element.17), channel_id=1, source_target_pairs={{1,0},{3,2},{5,4},{7,6},{9,8},{11,10},{13,12},{15,14},{17,16},{19,... | collective-permute-start | bytes 202760 | tf_op jit(solution)/shard_map/ppermute | solution.py:403
  90.5 3.9 %collective-permute-start.3 = (bf16[132,2,128]{2,1,0:T(2,128)(2,1)S(1)}, bf16[132,2,128]{2,1,0:T(2,128)(2,1)S(1)}, u32[]{:S(2)}, u32[]{:S(2)}) collective-permute-start(bf16[132,2,128]{2,1,0:T(2,128)(2,1)S(1)} %get-tuple-element.18), channel_id=1, source_target_pairs={{0,1},{2,3},{4,5},{6,7},{8,9},{10,11},{12,13},{14,15},{16,17},{18,... | collective-permute-start | bytes 202760 | tf_op jit(solution)/shard_map/ppermute | solution.py:402

commit v3 on v2

--- a/solution.py
+++ b/solution.py
@@ -247,7 +247,7 @@
     cells, entries, _ = weight.shape
     channels = blocks.shape[2]
     tile_cells = AR * fine_cols
-    per_step = 2
+    per_step = 4
     step_cells = per_step * tile_cells
     smem = pl.BlockSpec(memory_space=pltpu.SMEM)
     vmem = pl.BlockSpec(memory_space=pltpu.VMEM)
@@ -379,7 +379,7 @@
     width = fine_cols + SIDE
     vmem = pl.BlockSpec(memory_space=pltpu.VMEM)
     return pl.pallas_call(
-        functools.partial(conv_kernel, rows_one=10, rows_two=8),
+        functools.partial(conv_kernel, rows_one=10, rows_two=16),
         out_shape=jax.ShapeDtypeStruct(active.shape, jnp.bfloat16),
         in_specs=[vmem] * 9,
         out_specs=vmem,

time: 129 us -> 126 us (0.977)
  Pallas kernels: 102 us -> 99.1 us
    pallas_call x1, Pallas kernels: 32.5 us -> 30.9 us  [convolutions(): pl.pallas_call(functools.partial(conv_kernel, rows_one=10, rows_two=16),...]
    pallas_call x1, Pallas kernels: 41.3 us -> 39.8 us  [attend(): pl.pallas_call(functools.partial(attend_kernel, per_step=per_step, entrie...]
where the time goes in v3:
time: 126 us; the launch traced here: 125 us
  Pallas kernels  99.1 us (79%)
  local copies, waits for them, and re-layouts  11.1 us (9%)
  starting transfers between devices  9.04 us (7%)
  waiting for transfers between devices  4.47 us (4%)
    pallas_call x1, Pallas kernels, attend(): pl.pallas_call(functools.partial(attend_kernel, per_step=per_step, entrie...  39.8 us
    pallas_call x1, Pallas kernels, convolutions(): pl.pallas_call(functools.partial(conv_kernel, rows_one=10, rows_two=16),...  30.9 us
    pallas_call x1, Pallas kernels, gather(): pl.pallas_call(gather_kernel, out_shape=(jax.ShapeDtypeStruct((ring * coa...  28.3 us
    unnamed x22, local copies, waits for them, and re-layouts  8.66 us
    ppermute x2, starting transfers between devices, from_both(): before = lax.ppermute(tail, axis, [(i, i + 1) for i in range(ends)])  6.45 us
    ppermute x2, waiting for transfers between devices, from_both(): after = lax.ppermute(head, axis, [(i + 1, i) for i in range(ends)])  3.68 us
    ppermute x2, starting transfers between devices, from_both(): after = lax.ppermute(head, axis, [(i + 1, i) for i in range(ends)])  2.58 us
  transfers between devices with their start and end apart: 4, of which 2 were waited for; matrix products, arithmetic and copies ran while one was open for 1% of the time, Pallas kernels for 0%

profile of v3, /device:TPU:0, one launch (start us, length us, event | category | flops | bytes accessed | tf_op | source)
XLA Modules:
  0.0 125.0 jit_solution(14852300772543478256)
XLA Ops:
  0.0 0.8 copy.17
  0.8 0.1 reshape.32.wanted
  0.8 0.8 copy.18
  1.6 0.1 reshape.33.lists
  1.7 28.3 %gather.1 = (bf16[64,128,128]{2,1,0:T(8,128)(2,1)}, bf16[8,512,128]{2,1,0:T(8,128)(2,1)}) custom-call(bf16[8,128,128]{2,1,0:T(8,128)(2,1)} %coarse.1, bf16[4,512,128]{2,1,0:T(8,128)(2,1)} %patch.1), custom_call_target="tpu_custom_call" | custom-call | tf_op jit(solution)/shard_map/gather/pallas_call | solution.py:129
  30.0 0.0 copy-start
  30.0 1.6 %copy-done = bf16[64,128,128]{2,1,0:T(8,128)(2,1)S(1)} copy-done((bf16[64,128,128]{2,1,0:T(8,128)(2,1)S(1)}, bf16[64,128,128]{2,1,0:T(8,128)(2,1)}, u32[]{:S(2)}) %copy-start) | copy-done | bytes 2097176
  31.6 0.0 copy-start.1
  31.6 1.2 copy-done.1
  32.8 0.0 copy-start.2
  32.8 0.8 copy-done.2
  33.7 0.0 copy-start.3
  33.7 0.8 copy-done.3
  34.4 0.0 copy-start.4
  34.4 0.8 copy-done.4
  35.2 0.0 copy-start.5
  35.2 0.7 copy-done.5
  35.9 0.0 copy-start.6
  35.9 0.7 copy-done.6
  36.5 0.0 copy-start.7
  36.5 0.7 copy-done.7
  37.2 39.8 %attend.1 = (bf16[16384,128]{1,0:T(8,128)(2,1)}, bf16[16384,128]{1,0:T(8,128)(2,1)}) custom-call(s32[16]{0:T(128)S(1)} %reshape.32.wanted, s32[256]{0:T(256)S(1)} %reshape.33.lists, s32[64]{0:T(128)S(1)} %bitcast.14, s32[32]{0:T(128)S(1)} %bitcast.15, bf16[16384,4,128]{2,1,0:T(4,128)(2,1)} %bitcast.17, bf16[64,128,128]{2,1,0:T(8,128)(2,1)S(1)} %copy-done, ...), custom_call_target="tpu_custom_call" | custom-call | tf_op jit(solution)/shard_map/attend/pallas_call | solution.py:256
  77.0 0.9 fusion.1
  77.9 3.4 %collective-permute-start = (bf16[2,128,128]{2,1,0:T(8,128)(2,1)S(1)}, bf16[2,128,128]{2,1,0:T(8,128)(2,1)S(1)}, u32[]{:S(2)}, u32[]{:S(2)}) collective-permute-start(bf16[2,128,128]{2,1,0:T(8,128)(2,1)S(1)} %bitcast.22), channel_id=1, source_target_pairs={{0,2},{2,4},{4,6},{6,8},{8,10},{10,12},{12,14},{1,3},{3,5},{5,7},{... | collective-permute-start | bytes 196616 | tf_op jit(solution)/shard_map/ppermute | solution.py:402
  81.3 1.3 %collective-permute-start.1 = (bf16[2,128,128]{2,1,0:T(8,128)(2,1)S(1)}, bf16[2,128,128]{2,1,0:T(8,128)(2,1)S(1)}, u32[]{:S(2)}, u32[]{:S(2)}) collective-permute-start(bf16[2,128,128]{2,1,0:T(8,128)(2,1)S(1)} %bitcast.21), channel_id=1, source_target_pairs={{2,0},{4,2},{6,4},{8,6},{10,8},{12,10},{14,12},{3,1},{5,3},{7,5},{... | collective-permute-start | bytes 196616 | tf_op jit(solution)/shard_map/ppermute | solution.py:403
  82.6 1.1 fusion
  83.8 0.0 collective-permute-done.above
  83.8 0.0 copy-start.8
  83.8 3.7 %collective-permute-done.1.below = bf16[2,128,128]{2,1,0:T(8,128)(2,1)S(1)} collective-permute-done((bf16[2,128,128]{2,1,0:T(8,128)(2,1)S(1)}, bf16[2,128,128]{2,1,0:T(8,128)(2,1)S(1)}, u32[]{:S(2)}, u32[]{:S(2)}) %collective-permute-start.1) | collective-permute-done | bytes 65568 | tf_op jit(solution)/shard_map/ppermute | solution.py:403
  87.5 0.0 copy-start.9
  87.5 0.1 maximum_maximum_fusion
  87.6 0.1 fusion.2
  87.7 1.3 %collective-permute-start.2 = (bf16[132,2,128]{2,1,0:T(2,128)(2,1)S(1)}, bf16[132,2,128]{2,1,0:T(2,128)(2,1)S(1)}, u32[]{:S(2)}, u32[]{:S(2)}) collective-permute-start(bf16[132,2,128]{2,1,0:T(2,128)(2,1)S(1)} %get-tuple-element.17), channel_id=1, source_target_pairs={{1,0},{3,2},{5,4},{7,6},{9,8},{11,10},{13,12},{15,14},{17,16},{19,... | collective-permute-start | bytes 202760 | tf_op jit(solution)/shard_map/ppermute | solution.py:403
  89.0 3.0 %collective-permute-start.3 = (bf16[132,2,128]{2,1,0:T(2,128)(2,1)S(1)}, bf16[132,2,128]{2,1,0:T(2,128)(2,1)S(1)}, u32[]{:S(2)}, u32[]{:S(2)}) collective-permute-start(bf16[132,2,128]{2,1,0:T(2,128)(2,1)S(1)} %get-tuple-element.18), channel_id=1, source_target_pairs={{0,1},{2,3},{4,5},{6,7},{8,9},{10,11},{12,13},{14,15},{16,17},{18,... | collective-permute-start | bytes 202760 | tf_op jit(solution)/shard_map/ppermute | solution.py:402
  92.1 0.1 pad.1.clone
  92.2 0.0 collective-permute-done.2
  92.2 0.8 collective-permute-done.3
  93.0 1.1 pad_maximum_fusion.side
  94.0 0.0 copy-done.8
  94.0 0.0 copy-done.9
  94.0 30.9 %convolutions.1 = bf16[128,128,128]{2,1,0:T(8,128)(2,1)} custom-call(bf16[128,128,128]{2,1,0:T(8,128)(2,1)} %bitcast.19, bf16[2,128,128]{2,1,0:T(8,128)(2,1)} %copy-done.8, bf16[2,128,128]{2,1,0:T(8,128)(2,1)} %copy-done.9, bf16[132,16,128]{2,1,0:T(8,128)(2,1)} %pad_maximum_fusion.side, bf16[128,128,128]{2,1,0:T(8,128)(2,1)} %bitcast.20, ...), custom_call_target="tpu_custom_call" | custom-call | tf_op jit(solution)/shard_map/convolutions/pallas_call | solution.py:381
  (3 shorter events, 0.0 us)
Async XLA Ops:
  30.0 1.6 %copy-start = (bf16[64,128,128]{2,1,0:T(8,128)(2,1)S(1)}, bf16[64,128,128]{2,1,0:T(8,128)(2,1)}, u32[]{:S(2)}) copy-start(bf16[64,128,128]{2,1,0:T(8,128)(2,1)} %get-tuple-element.9.blocks) | copy-start | bytes 6291460
  31.6 1.2 copy-start.1
  32.8 0.8 copy-start.2
  33.7 0.8 copy-start.3
  34.4 0.8 copy-start.4
  35.2 0.7 copy-start.5
  35.9 0.7 copy-start.6
  36.5 0.7 copy-start.7
  77.9 5.9 %collective-permute-start = (bf16[2,128,128]{2,1,0:T(8,128)(2,1)S(1)}, bf16[2,128,128]{2,1,0:T(8,128)(2,1)S(1)}, u32[]{:S(2)}, u32[]{:S(2)}) collective-permute-start(bf16[2,128,128]{2,1,0:T(8,128)(2,1)S(1)} %bitcast.22), channel_id=1, source_target_pairs={{0,2},{2,4},{4,6},{6,8},{8,10},{10,12},{12,14},{1,3},{3,5},{5,7},{... | collective-permute-start | bytes 196616 | tf_op jit(solution)/shard_map/ppermute | solution.py:402
  81.3 6.2 %collective-permute-start.1 = (bf16[2,128,128]{2,1,0:T(8,128)(2,1)S(1)}, bf16[2,128,128]{2,1,0:T(8,128)(2,1)S(1)}, u32[]{:S(2)}, u32[]{:S(2)}) collective-permute-start(bf16[2,128,128]{2,1,0:T(8,128)(2,1)S(1)} %bitcast.21), channel_id=1, source_target_pairs={{2,0},{4,2},{6,4},{8,6},{10,8},{12,10},{14,12},{3,1},{5,3},{7,5},{... | collective-permute-start | bytes 196616 | tf_op jit(solution)/shard_map/ppermute | solution.py:403
  83.8 10.3 %copy-start.8 = (bf16[2,128,128]{2,1,0:T(8,128)(2,1)}, bf16[2,128,128]{2,1,0:T(8,128)(2,1)S(1)}, u32[]{:S(2)}) copy-start(bf16[2,128,128]{2,1,0:T(8,128)(2,1)S(1)} %collective-permute-done.above) | copy-start | bytes 196612
  87.5 6.6 %copy-start.9 = (bf16[2,128,128]{2,1,0:T(8,128)(2,1)}, bf16[2,128,128]{2,1,0:T(8,128)(2,1)S(1)}, u32[]{:S(2)}) copy-start(bf16[2,128,128]{2,1,0:T(8,128)(2,1)S(1)} %collective-permute-done.1.below) | copy-start | bytes 196612
  87.7 4.4 %collective-permute-start.2 = (bf16[132,2,128]{2,1,0:T(2,128)(2,1)S(1)}, bf16[132,2,128]{2,1,0:T(2,128)(2,1)S(1)}, u32[]{:S(2)}, u32[]{:S(2)}) collective-permute-start(bf16[132,2,128]{2,1,0:T(2,128)(2,1)S(1)} %get-tuple-element.17), channel_id=1, source_target_pairs={{1,0},{3,2},{5,4},{7,6},{9,8},{11,10},{13,12},{15,14},{17,16},{19,... | collective-permute-start | bytes 202760 | tf_op jit(solution)/shard_map/ppermute | solution.py:403
  89.0 3.9 %collective-permute-start.3 = (bf16[132,2,128]{2,1,0:T(2,128)(2,1)S(1)}, bf16[132,2,128]{2,1,0:T(2,128)(2,1)S(1)}, u32[]{:S(2)}, u32[]{:S(2)}) collective-permute-start(bf16[132,2,128]{2,1,0:T(2,128)(2,1)S(1)} %get-tuple-element.18), channel_id=1, source_target_pairs={{0,1},{2,3},{4,5},{6,7},{8,9},{10,11},{12,13},{14,15},{16,17},{18,... | collective-permute-start | bytes 202760 | tf_op jit(solution)/shard_map/ppermute | solution.py:402
